TPU v7x, 32 devices: a whole 2x2x4 slice. The times are simulated.
32 devices in a mesh: depth: 4 (over y, x), tile: 8 (over z, core).
Axes of the slice: x: 2, y: 2, z: 4, core: 2. Of those that a mesh axis runs over, the one named last changes fastest.
Arguments:
- density: float32 [128, 256, 2048], P('depth', 'tile'), may hold values from 0 to 1
- palette: float32 [2, 3], replicated, may hold values from 0.2 to 1
- light_dir: float32 [2, 3], replicated, may hold values from -4 to 4
- slab_of: int32 [4], replicated, may hold values from 0 to 3, each once
Outputs:
- images: float32 [2, 4, 256, 2048], P(None, None, 'tile', 'depth')
Inputs may be any that keep to these rules, and one draw needn't show every extreme that they name: `slab_of`: each of 0 to 3 appears once.
All inputs are finite; a program needn't handle non-finite values.
Results may differ from a plain program's by a relative error of at most 0.0008.
Values may be sent and summed in bfloat16 or wider, within the bound.
A program may use at most 128 MiB of HBM per device.

v0:
```python
import jax
import jax.numpy as jnp
from jax import lax
from jax.sharding import PartitionSpec as P

HIGH = lax.Precision.HIGHEST


def padded_2(block, sides, width):
    for axis, dim in sides:
        count = lax.axis_size(axis)
        forward = [(i, i + 1) for i in range(count - 1)]
        backward = [(target, source) for source, target in forward]
        low = lax.ppermute(
            lax.slice_in_dim(block, block.shape[dim] - width, None, axis=dim), axis, forward
        )
        high = lax.ppermute(lax.slice_in_dim(block, 0, width, axis=dim), axis, backward)
        block = jnp.concatenate([low, block, high], axis=dim)
    return block


def centred(field, axis):
    size = field.shape[axis]
    upper = jnp.concatenate(
        [
            lax.slice_in_dim(field, 1, size, axis=axis),
            lax.slice_in_dim(field, size - 1, size, axis=axis),
        ],
        axis,
    )
    lower = jnp.concatenate(
        [lax.slice_in_dim(field, 0, 1, axis=axis), lax.slice_in_dim(field, 0, size - 1, axis=axis)],
        axis,
    )
    return (upper - lower) * 0.5


def march(block, grad_x, palette, light_dir, factor):
    grad_z = centred(block, 0)
    grad_y = centred(block, 2)
    length = jnp.sqrt(grad_x * grad_x + grad_y * grad_y + grad_z * grad_z + 0.25)
    optical = block * factor
    opacity = 1.0 - jnp.exp(-optical)
    running = jnp.cumsum(optical, axis=0)
    slab_tau = running[-1]
    before = [running - optical, slab_tau[None] - running]
    colours = []
    for view in range(2):
        facing = (
            grad_x * light_dir[view, 0] + grad_y * light_dir[view, 1] + grad_z * light_dir[view, 2]
        )
        shade = 0.3 + jnp.abs(facing) / length
        weight = opacity * jnp.exp(-before[view]) * shade
        plain = jnp.sum(weight, axis=0)
        dense = jnp.sum(block * weight, axis=0)
        colours.append(
            palette[0][:, None, None] * plain[None] + palette[1][:, None, None] * dense[None]
        )
    return (jnp.stack(colours).astype(jnp.bfloat16), slab_tau.astype(jnp.bfloat16))


def compose(slab_rgb, slab_tau, slab_of):
    tau_full = slab_tau.astype(jnp.float32)
    earlier = (slab_of[None, :] < slab_of[:, None]).astype(jnp.float32)
    later = (slab_of[None, :] > slab_of[:, None]).astype(jnp.float32)
    front_one = jnp.einsum("jk,kxy->jxy", earlier, tau_full, precision=HIGH)
    front_two = jnp.einsum("jk,kxy->jxy", later, tau_full, precision=HIGH)
    rgb_full = slab_rgb.astype(jnp.float32)
    colour_one = jnp.einsum("jcxy,jxy->cxy", rgb_full[:, 0], jnp.exp(-front_one), precision=HIGH)
    colour_two = jnp.einsum("jcxy,jxy->cxy", rgb_full[:, 1], jnp.exp(-front_two), precision=HIGH)
    coverage = 1.0 - jnp.exp(-jnp.sum(tau_full, axis=0))
    return jnp.stack(
        [
            jnp.concatenate([colour_one, coverage[None]], 0),
            jnp.concatenate([colour_two, coverage[None]], 0),
        ]
    )


def on_device(density, palette, light_dir, slab_of):
    slab_rows, tile_rows, image_cols = density.shape
    depth_count = lax.axis_size("depth")
    tile_count = lax.axis_size("tile")
    tile_place = lax.axis_index("tile")
    padded = padded_2(density, (("tile", 1),), 1)
    left_plane = jnp.where(tile_place == 0, density[:, :1], padded[:, :1])
    right_plane = jnp.where(tile_place == tile_count - 1, density[:, -1:], padded[:, -1:])
    full_x = jnp.concatenate([left_plane, density, right_plane], axis=1)
    grad_x = (full_x[:, 2:] - full_x[:, :-2]) * 0.5
    factor = 3.0 / (slab_rows * depth_count)
    slab_rgb, slab_tau = march(density, grad_x, palette, light_dir, factor)
    return compose(
        lax.all_to_all(slab_rgb[None], "depth", split_axis=4, concat_axis=0, tiled=True),
        lax.all_to_all(
            slab_tau[None, None, None], "depth", split_axis=4, concat_axis=0, tiled=True
        )[:, 0, 0],
        slab_of,
    )


def solution(mesh):
    in_specs = (P("depth", "tile", None), P(), P(), P())
    out_specs = P(None, None, "tile", "depth")
    return jax.shard_map(
        on_device, mesh=mesh, in_specs=in_specs, out_specs=out_specs, check_vma=False
    )
```

profile of v0, /device:TPU:0, one launch (start us, length us, event | category | flops | bytes accessed | tf_op | source)
XLA Modules:
  0.0 162.5 jit_solution(15282459363919092748)
XLA Ops:
  0.0 2.7 %fusion.29 = (f32[32,1,2048]{2,1,0:T(1,128)S(1)}, f32[32,1,2048]{2,1,0:T(1,128)S(1)}) fusion(f32[32,32,2048]{2,1,0:T(8,128)} %param.4), kind=kLoop, calls=%fused_computation.57 | loop fusion | bytes 1048576 | tf_op jit(solution)/shard_map/slice | solution.py:86
  2.7 1.3 collective-permute-start
  4.0 3.0 %collective-permute-start.1 = (f32[32,1,2048]{2,1,0:T(1,128)S(1)}, f32[32,1,2048]{2,1,0:T(1,128)S(1)}, u32[]{:S(2)}, u32[]{:S(2)}) collective-permute-start(f32[32,1,2048]{2,1,0:T(1,128)S(1)} %get-tuple-element.20), channel_id=1, source_target_pairs={{0,1},{1,2},{2,3},{3,4},{4,5},{5,6},{6,7},{8,9},{9,10},{10,11},{11... | collective-permute-start | bytes 786440 | tf_op jit(solution)/shard_map/ppermute | solution.py:14
  7.0 0.0 slice-start
  7.0 0.0 slice-start.1
  7.1 13.2 %fusion.25 = (f32[32,32,2047]{2,1,0:T(8,128)}, f32[32,32,2047]{2,1,0:T(8,128)}) fusion(f32[32,32,2048]{2,1,0:T(8,128)} %param.4), kind=kLoop, calls=%fused_computation.53 | loop fusion | bytes 33538048 | tf_op jit(solution)/shard_map/slice | solution.py:26
  20.3 0.0 slice-done
  20.3 0.0 slice-done.1
  20.3 0.0 copy-start
  20.3 0.0 copy-start.2
  20.3 6.2 %fusion.27 = (f32[31,32,2048]{2,1,0:T(8,128)}, f32[31,32,2048]{2,1,0:T(8,128)}) fusion(f32[32,32,2048]{2,1,0:T(8,128)S(1)} %bitcast.65), kind=kLoop, calls=%fused_computation.55 | loop fusion | bytes 32505856 | tf_op jit(solution)/shard_map/slice | solution.py:26
  26.5 0.0 copy-done
  26.5 0.7 fusion.31
  31.1 1.4 fusion.26
  32.5 0.0 collective-permute-done
  32.5 0.0 collective-permute-done.1
  32.5 2.9 %broadcast_select_fusion.1 = (f32[32,1,2048]{2,1,0:T(1,128)S(1)}, f32[32,1,2048]{2,1,0:T(1,128)S(1)}) fusion(f32[32,1,2048]{2,1,0:T(1,128)S(1)} %collective-permute-done, pred[]{:T(512)S(6)} %eq.6, f32[32,32,2048]{2,1,0:T(8,128)} %param.4, f32[32,1,2048]{2,1,0:T(1,128)S(1)} %collective-permute-done.1, pred[]{:T(512)S(6)} %eq.7), kind=kLoop, calls=%fused_computation.27 | loop fusion | flops 131072 | bytes 1572866 | tf_op jit(solution)/shard_map/jit(_where)/select_n | solution.py:87
  35.4 30.6 %add_multiply_fusion.1 = (f32[32,32,2048]{2,1,0:T(8,128)}, f32[32,32,2048]{2,1,0:T(8,128)}) fusion(f32[32,32,2048]{2,1,0:T(8,128)} %param.4, f32[32,1,2048]{2,1,0:T(1,128)S(1)} %get-tuple-element.18, f32[32,1,2048]{2,1,0:T(1,128)S(1)} %get-tuple-element.17, f32[]{:T(128)} %bitcast.11, f32[]{:T(128)} %bitcast.10, f32[]{:T(128)} %bitcast.9, ...), kind=kOutput, calls=%fused_computation.8 | output fusion | flops 136314880 | bytes 59244556 | tf_op jit(solution)/shard_map/jit(cumsum)/reduce_window_sum | solution.py:44
  66.0 1.0 slice_bitcast_fusion
  67.0 1.0 fusion.12
  68.0 0.7 copy.16
  68.7 0.6 broadcast.143
  69.3 12.5 %reduce.4 = bf16[2048,32]{1,0:T(8,128)(2,1)} reduce(bf16[2048,1,1,1,32]{4,3,2,1,0:T(2,128)(2,1)S(1)} %bitcast.69, bf16[]{:T(256)} %broadcast.143), dimensions={1,2,3}, to_apply=%bitcast.60.reduce_sub_computation | reduce | bytes 262146
  81.8 2.2 %reshape.92 = bf16[4,2,8192]{2,1,0:T(2,128)(2,1)} reshape(bf16[2048,32]{1,0:T(8,128)(2,1)} %reduce.4) | data formatting | bytes 262144
  84.0 5.2 %all-to-all-start = ((bf16[4,2,8192]{2,1,0:T(2,128)(2,1)}), bf16[4,2,8192]{2,1,0:T(2,128)(2,1)S(1)}, u32[]{:S(2)}, u32[]{:S(2)}) async-start(bf16[4,2,8192]{2,1,0:T(2,128)(2,1)} %reshape.92), calls=%async_computation | async-start | bytes 262144 | tf_op jit(solution)/shard_map/all_to_all | solution.py:94
  89.2 31.4 %fusion.24 = (f32[32,2048]{1,0:T(8,128)S(1)}, f32[32,2048]{1,0:T(8,128)S(1)}, f32[32,2048]{1,0:T(8,128)S(1)}, f32[32,2048]{1,0:T(8,128)S(1)}) fusion(f32[32,32,2048]{2,1,0:T(8,128)} %get-tuple-element.35, f32[32,32,2048]{2,1,0:T(8,128)} %param.4, f32[]{:T(128)} %bitcast.17, f32[31,32,2048]{2,1,0:T(8,128)} %get-tuple-element.14, ...), kind=kLoop, calls=%fused_computation.52 | loop fusion | flops 81526784 | bytes 60555276 | tf_op jit(solution)/shard_map/reduce_sum | solution.py:54
  120.6 0.0 copy-start.1
  120.6 0.3 fusion.8
  120.8 1.0 pad_maximum_fusion.2
  121.8 7.5 %copy.18 = bf16[1,2,3,32,2048]{3,1,2,0,4:T(2,128)(2,1)S(1)} copy(bf16[1,2,3,32,2048]{4,3,2,1,0:T(8,128)(2,1)} %pad_maximum_fusion.2) | data formatting | bytes 1572864 | tf_op jit(solution)/shard_map/stack | solution.py:59
  129.4 3.8 %reshape.94 = bf16[4,2,49152]{2,1,0:T(2,128)(2,1)} reshape(bf16[2048,1,3,2,32]{4,3,2,1,0:T(2,128)(2,1)S(1)} %bitcast.66) | data formatting | bytes 1572864
  133.2 0.0 all-to-all-done
  133.2 4.2 %all-to-all-start.1 = ((bf16[4,2,49152]{2,1,0:T(2,128)(2,1)}), bf16[4,2,49152]{2,1,0:T(2,128)(2,1)}, u32[]{:S(2)}, u32[]{:S(2)}) async-start(bf16[4,2,49152]{2,1,0:T(2,128)(2,1)} %reshape.94), calls=%async_computation.1 | async-start | bytes 1572864 | tf_op jit(solution)/shard_map/all_to_all | solution.py:93
  137.4 0.7 reshape.93
  138.1 0.5 copy.17
  138.6 0.1 all_to_all.25
  138.7 0.0 copy-done.1
  138.7 0.3 fusion.7
  139.0 0.1 copy.39
  139.1 0.3 fusion.5
  139.4 0.8 copy.40
  140.2 0.2 convert_reduce_fusion
  140.3 9.2 %all-to-all-done.1 = bf16[4,2,49152]{2,1,0:T(2,128)(2,1)} async-done(((bf16[4,2,49152]{2,1,0:T(2,128)(2,1)}), bf16[4,2,49152]{2,1,0:T(2,128)(2,1)}, u32[]{:S(2)}, u32[]{:S(2)}) %all-to-all-start.1) | async-done | bytes 786464 | tf_op jit(solution)/shard_map/all_to_all | solution.py:93
  149.6 3.2 %reshape.95 = bf16[2048,1,3,2,32]{4,3,2,1,0:T(2,128)(2,1)S(1)} reshape(bf16[4,2,49152]{2,1,0:T(2,128)(2,1)} %all-to-all-done.1) | data formatting | bytes 1572864
  152.8 6.2 %copy.36 = bf16[1,2,3,32,4,512]{5,4,3,2,1,0:T(4,128)(2,1)} copy(bf16[1,2,3,32,4,512]{3,1,2,5,4,0:T(2,128)(2,1)S(1)} %bitcast.67) | data formatting | bytes 1572864 | tf_op jit(solution)/shard_map/all_to_all | solution.py:93
  159.0 1.4 fusion.30
  160.4 1.2 multiply_reduce_fusion.2
  161.6 0.8 pad_maximum_fusion.3
  (6 shorter events, 0.1 us)
Async XLA Ops:
  2.7 29.8 %collective-permute-start = (f32[32,1,2048]{2,1,0:T(1,128)S(1)}, f32[32,1,2048]{2,1,0:T(1,128)S(1)}, u32[]{:S(2)}, u32[]{:S(2)}) collective-permute-start(f32[32,1,2048]{2,1,0:T(1,128)S(1)} %get-tuple-element.19), channel_id=1, source_target_pairs={{1,0},{2,1},{3,2},{4,3},{5,4},{6,5},{7,6},{9,8},{10,9},{11,10},{12... | collective-permute-start | bytes 786440 | tf_op jit(solution)/shard_map/ppermute | solution.py:17
  4.0 28.5 %collective-permute-start.1 = (f32[32,1,2048]{2,1,0:T(1,128)S(1)}, f32[32,1,2048]{2,1,0:T(1,128)S(1)}, u32[]{:S(2)}, u32[]{:S(2)}) collective-permute-start(f32[32,1,2048]{2,1,0:T(1,128)S(1)} %get-tuple-element.20), channel_id=1, source_target_pairs={{0,1},{1,2},{2,3},{3,4},{4,5},{5,6},{6,7},{8,9},{9,10},{10,11},{11... | collective-permute-start | bytes 786440 | tf_op jit(solution)/shard_map/ppermute | solution.py:14
  7.0 13.3 %slice-start = ((s8[8388608]{0:T(1024)(128)(4,1)}), s8[4194304]{0:T(1024)(128)(4,1)S(1)}, s32[]{:S(2)}) async-start(s8[8388608]{0:T(1024)(128)(4,1)} %bitcast.64), calls=%async_computation.2 | async-start | bytes 8388608
  7.0 13.2 %slice-start.1 = ((s8[8388608]{0:T(1024)(128)(4,1)}), s8[4194304]{0:T(1024)(128)(4,1)S(1)}, s32[]{:S(2)}) async-start(s8[8388608]{0:T(1024)(128)(4,1)} %bitcast.64), calls=%async_computation.3 | async-start | bytes 8388608
  20.3 6.2 %copy-start = (f32[2,3]{1,0:T(2,128)S(1)}, f32[2,3]{1,0:T(2,128)}, u32[]{:S(2)}) copy-start(f32[2,3]{1,0:T(2,128)} %param.6) | copy-start | bytes 76
  20.3 10.8 %copy-start.2 = (f32[2,3]{1,0:T(2,128)S(1)}, f32[2,3]{1,0:T(2,128)}, u32[]{:S(2)}) copy-start(f32[2,3]{1,0:T(2,128)} %param.5) | copy-start | bytes 76
  84.0 49.2 %all-to-all-start = ((bf16[4,2,8192]{2,1,0:T(2,128)(2,1)}), bf16[4,2,8192]{2,1,0:T(2,128)(2,1)S(1)}, u32[]{:S(2)}, u32[]{:S(2)}) async-start(bf16[4,2,8192]{2,1,0:T(2,128)(2,1)} %reshape.92), calls=%async_computation | async-start | bytes 262144 | tf_op jit(solution)/shard_map/all_to_all | solution.py:94
  120.6 18.1 %copy-start.1 = (s32[4]{0:T(128)S(1)}, s32[4]{0:T(128)}, u32[]{:S(2)}) copy-start(s32[4]{0:T(128)} %param.7) | copy-start | bytes 52
  133.2 16.4 %all-to-all-start.1 = ((bf16[4,2,49152]{2,1,0:T(2,128)(2,1)}), bf16[4,2,49152]{2,1,0:T(2,128)(2,1)}, u32[]{:S(2)}, u32[]{:S(2)}) async-start(bf16[4,2,49152]{2,1,0:T(2,128)(2,1)} %reshape.94), calls=%async_computation.1 | async-start | bytes 1572864 | tf_op jit(solution)/shard_map/all_to_all | solution.py:93
where the time goes:
time: 163 us; the launch traced here: 162 us
  other arithmetic  80.9 us (50%)
  local copies, waits for them, and re-layouts  54 us (33%)
  starting transfers between devices  13.7 us (8%)
  waiting for transfers between devices  9.26 us (6%)
  between operations  4.11 us (3%)
    reduce_sum x1, other arithmetic, march(): plain = jnp.sum(weight, axis=0)  31.4 us
    another operation x1, other arithmetic, march(): running = jnp.cumsum(optical, axis=0)  30.6 us
    slice x2, local copies, waits for them, and re-layouts, centred(): lax.slice_in_dim(field, 1, size, axis=axis)  19.4 us
    unnamed x2, other arithmetic  12.5 us
    unnamed x17, local copies, waits for them, and re-layouts  11.4 us
    all_to_all x1, waiting for transfers between devices, on_device(): lax.all_to_all(slab_rgb[None], 'depth', split_axis=4, concat_axis=0, tile...  9.25 us
    another operation x1, local copies, waits for them, and re-layouts, march(): jnp.stack(colours).astype(jnp.bfloat16)  7.54 us
    all_to_all x1, local copies, waits for them, and re-layouts, on_device(): lax.all_to_all(slab_rgb[None], 'depth', split_axis=4, concat_axis=0, tile...  6.17 us
  transfers between devices with their start and end apart: 4, of which 1 were waited for; matrix products, arithmetic and copies ran while one was open for 42% of the time, Pallas kernels for 0%

commit v1 on v0

v1 whole, which is shorter than its diff:
```python
import functools
import math

import jax
import jax.numpy as jnp
from jax import lax
from jax.experimental import pallas as pl
from jax.experimental.pallas import tpu as pltpu
from jax.sharding import PartitionSpec as P

LANES = 128
SUB = 8
UNIT = 16
PAD = 8


def partner(me, step, count):
    if count & (count - 1):
        return lax.rem(me + step, count)
    out, bit = 0, 1
    while bit < count:
        mine = lax.rem(me // bit, 2)
        out = out + bit * (1 - mine if step & bit else mine)
        bit *= 2
    return out


def kernel(
    geom, density, palette, light, slab_of, out, buf, stag, send, recv,
    load_sem, halo_send, halo_recv, send_sem, recv_sem,
):
    rows, xs, ncols, depth_n, tile_n, tiles_per, group, unroll = geom
    tiles = ncols // LANES
    me = lax.axis_index("depth")
    tile = lax.axis_index("tile")
    left = lax.rem(tile + tile_n - 1, tile_n)
    right = lax.rem(tile + 1, tile_n)
    barrier = pltpu.get_barrier_semaphore()
    for step in range(1, depth_n):
        pl.semaphore_signal(
            barrier, inc=1, device_id={"depth": partner(me, step, depth_n)},
            device_id_type=pl.DeviceIdType.MESH,
        )
    for side in (left, right):
        pl.semaphore_signal(
            barrier, inc=1, device_id={"tile": side}, device_id_type=pl.DeviceIdType.MESH
        )

    def load(j):
        return pltpu.make_async_copy(
            density.at[:, :, pl.ds(j * LANES, LANES)],
            buf.at[:, j, pl.ds(PAD, xs), :],
            load_sem.at[j],
        )

    for j in range(tiles):
        load(j).start()
    pl.semaphore_wait(barrier, depth_n + 1)

    low_row, high_row = PAD - 1, PAD + xs

    def halo_to(j, side, target):
        source, row = ((xs - 1, low_row), (0, high_row))[side]
        return pltpu.make_async_remote_copy(
            src_ref=density.at[:, pl.ds(source, 1), pl.ds(j * LANES, LANES)],
            dst_ref=buf.at[:, j, pl.ds(row, 1), :],
            send_sem=halo_send.at[side, j],
            recv_sem=halo_recv.at[side, j],
            device_id={"tile": target},
            device_id_type=pl.DeviceIdType.MESH,
        )

    def halo_own(j, side):
        source, row = ((0, low_row), (xs - 1, high_row))[side]
        return pltpu.make_async_copy(
            density.at[:, pl.ds(source, 1), pl.ds(j * LANES, LANES)],
            buf.at[:, j, pl.ds(row, 1), :],
            halo_recv.at[side, j],
        )

    @pl.when(tile < tile_n - 1)
    def _():
        for j in range(tiles):
            halo_to(j, 0, right).start()

    @pl.when(tile > 0)
    def _():
        for j in range(tiles):
            halo_to(j, 1, left).start()

    @pl.when(tile == 0)
    def _():
        for j in range(tiles):
            halo_own(j, 0).start()

    @pl.when(tile == tile_n - 1)
    def _():
        for j in range(tiles):
            halo_own(j, 1).start()

    for j in range(tiles):
        load(j).wait()

    factor = 3.0 / (rows * depth_n)
    scale = factor * math.log2(math.e)
    lights = [[light[v, c] for c in range(3)] for v in range(2)]
    colours = [[palette[a, c] for c in range(3)] for a in range(2)]
    lane = lax.broadcasted_iota(jnp.int32, (group, SUB, LANES), 2)
    place = lax.broadcasted_iota(jnp.int32, (group, SUB, LANES), 0)
    first, last = lane == 0, lane == LANES - 1

    def sweep(j0, x0, stag_j, stag_row):
        end_low = first & (place == 0) & (j0 == 0)
        end_high = last & (place == group - 1) & (j0 + group == tiles)
        j_low = jnp.maximum(j0 - 1, 0)
        j_high = jnp.minimum(j0 + group, tiles - 1)
        here = pl.ds(pl.multiple_of(x0 + PAD, SUB), SUB)

        def at(z, offset=0):
            return buf[z, pl.ds(j0, group), pl.ds(x0 + PAD + offset, SUB), :]

        def block(step, carry):
            run, seen, grown, p0, d0, p1, d1 = carry
            z0 = step * unroll
            below = at(jnp.maximum(z0 - 1, 0))
            mid = at(z0)
            for i in range(unroll):
                z = z0 + i
                above = at(jnp.minimum(z + 1, rows - 1) if i == unroll - 1 else z + 1)
                gz = above - below
                gx = at(z, 1) - at(z, -1)
                edge_low = buf[z, pl.ds(j_low, 1), here, :]
                edge_high = buf[z, pl.ds(j_high, 1), here, :]
                if group > 1:
                    edge_low = jnp.concatenate([edge_low, mid[:-1]], 0)
                    edge_high = jnp.concatenate([mid[1:], edge_high], 0)
                prior = pltpu.roll(jnp.where(last, edge_low, mid), 1, 2)
                after = pltpu.roll(jnp.where(first, edge_high, mid), LANES - 1, 2)
                prior = jnp.where(end_low, mid, prior)
                after = jnp.where(end_high, mid, after)
                gy = after - prior
                inverse = lax.rsqrt(gx * gx + gy * gy + (gz * gz + 1.0))
                shades = [
                    jnp.abs(gx * l[0] + gy * l[1] + gz * l[2]) * inverse + 0.3 for l in lights
                ]
                run = run + mid
                power = run * scale
                seen_next = jnp.exp2(-power)
                grown_next = jnp.exp2(power)
                c0 = (seen - seen_next) * shades[0]
                c1 = (grown_next - grown) * shades[1]
                p0 = p0 + c0
                d0 = d0 + mid * c0
                p1 = p1 + c1
                d1 = d1 + mid * c1
                seen, grown = seen_next, grown_next
                below, mid = mid, above
            return run, seen, grown, p0, d0, p1, d1

        zero = jnp.zeros((group, SUB, LANES), jnp.float32)
        one = jnp.ones((group, SUB, LANES), jnp.float32)
        run, seen, _, p0, d0, p1, d1 = lax.fori_loop(
            0, rows // unroll, block, (zero, one, one, zero, zero, zero, zero)
        )
        p1, d1 = p1 * seen, d1 * seen
        fields = [colours[0][c] * p0 + colours[1][c] * d0 for c in range(3)]
        fields += [colours[0][c] * p1 + colours[1][c] * d1 for c in range(3)]
        fields.append(run * factor)
        for f, value in enumerate(fields):
            stag[f, pl.ds(stag_j, group), pl.ds(pl.multiple_of(stag_row, SUB), SUB), :] = value

    groups = tiles_per // group

    def unit(dest, x_first, x_step, target):
        def part(index, _):
            half, piece = index // groups, lax.rem(index, groups)
            sweep(
                dest * tiles_per + piece * group, x_first + half * x_step, piece * group, half * SUB
            )
            return 0

        lax.fori_loop(0, 2 * groups, part, 0)
        for f in range(7):
            for j in range(tiles_per):
                target[f, :, pl.ds(j * LANES, LANES)] = stag[f, j].astype(jnp.bfloat16)

    def outgoing(step, u):
        return pltpu.make_async_remote_copy(
            src_ref=send.at[step - 1, u],
            dst_ref=recv.at[me, u],
            send_sem=send_sem.at[step - 1, u],
            recv_sem=recv_sem.at[me, u],
            device_id={"depth": partner(me, step, depth_n)},
            device_id_type=pl.DeviceIdType.MESH,
        )

    def incoming(source, u):
        return pltpu.make_async_remote_copy(
            src_ref=send.at[0, u],
            dst_ref=recv.at[source, u],
            send_sem=send_sem.at[0, u],
            recv_sem=recv_sem.at[source, u],
            device_id={"depth": source},
            device_id_type=pl.DeviceIdType.MESH,
        )

    pairs = xs // UNIT
    for u in range(pairs):
        if u == pairs - 1:
            for j in range(tiles):
                for side, has in ((0, tile > 0), (1, tile < tile_n - 1)):

                    @pl.when(has)
                    def _(j=j, side=side):
                        halo_to(j, side, (right, left)[side]).wait_recv()

                    @pl.when(jnp.logical_not(has))
                    def _(j=j, side=side):
                        halo_own(j, side).wait()

        if u == pairs - 1:
            x_first, x_step = 0, xs - SUB
        else:
            x_first, x_step = SUB + u * UNIT, SUB
        for step in range(depth_n - 1, 0, -1):
            unit(partner(me, step, depth_n), x_first, x_step, send.at[step - 1, u])
            outgoing(step, u).start()
        unit(me, x_first, x_step, recv.at[me, u])

    order = [slab_of[k] for k in range(depth_n)]
    for u in range(pairs):
        for step in range(1, depth_n):
            incoming(partner(me, step, depth_n), u).wait_recv()
        if u == pairs - 1:
            x_first, x_step = 0, xs - SUB
        else:
            x_first, x_step = SUB + u * UNIT, SUB

        def compose(j, _):
            cols = pl.ds(pl.multiple_of(j * LANES, LANES), LANES)
            taus = [recv[k, u, 6, :, cols].astype(jnp.float32) for k in range(depth_n)]
            total = functools.reduce(jnp.add, taus)
            coverage = 1.0 - jnp.exp(-total)
            sums = [[0.0] * 3 for _ in range(2)]
            for b in range(depth_n):
                front = jnp.zeros_like(total)
                behind = jnp.zeros_like(total)
                for k in range(depth_n):
                    if k != b:
                        front += jnp.where(order[k] < order[b], 1.0, 0.0) * taus[k]
                        behind += jnp.where(order[k] > order[b], 1.0, 0.0) * taus[k]
                for v, depth in enumerate((front, behind)):
                    fade = jnp.exp(-depth)
                    for c in range(3):
                        value = recv[b, u, 3 * v + c, :, cols].astype(jnp.float32)
                        sums[v][c] = sums[v][c] + value * fade
            for v in range(2):
                for c, value in enumerate(sums[v] + [coverage]):
                    for half in range(2):
                        out[v, c, pl.ds(x_first + half * x_step, SUB), cols] = value[
                            half * SUB : (half + 1) * SUB
                        ]
            return 0

        lax.fori_loop(0, tiles_per, compose, 0)

    for u in range(pairs):
        for step in range(1, depth_n):
            outgoing(step, u).wait_send()
    for j in range(tiles):

        @pl.when(tile < tile_n - 1)
        def _(j=j):
            halo_to(j, 0, right).wait_send()

        @pl.when(tile > 0)
        def _(j=j):
            halo_to(j, 1, left).wait_send()


def on_device(depth_n, tile_n, density, palette, light_dir, slab_of):
    rows, xs, ncols = density.shape
    tiles = ncols // LANES
    tiles_per = tiles // depth_n
    group = 2 if tiles_per % 2 == 0 else 1
    unroll = 16
    geom = (rows, xs, ncols, depth_n, tile_n, tiles_per, group, unroll)
    pairs = xs // UNIT
    cols = ncols // depth_n
    smem = pl.BlockSpec(memory_space=pltpu.SMEM)
    return pl.pallas_call(
        functools.partial(kernel, geom),
        out_shape=jax.ShapeDtypeStruct((2, 4, xs, cols), jnp.float32),
        in_specs=[pl.BlockSpec(memory_space=pl.ANY), smem, smem, smem],
        out_specs=pl.BlockSpec(memory_space=pltpu.VMEM),
        scratch_shapes=[
            pltpu.VMEM((rows, tiles, xs + 2 * PAD, LANES), jnp.float32),
            pltpu.VMEM((7, tiles_per, UNIT, LANES), jnp.float32),
            pltpu.VMEM((depth_n - 1, pairs, 7, UNIT, cols), jnp.bfloat16),
            pltpu.VMEM((depth_n, pairs, 7, UNIT, cols), jnp.bfloat16),
            pltpu.SemaphoreType.DMA((tiles,)),
            pltpu.SemaphoreType.DMA((2, tiles)),
            pltpu.SemaphoreType.DMA((2, tiles)),
            pltpu.SemaphoreType.DMA((depth_n - 1, pairs)),
            pltpu.SemaphoreType.DMA((depth_n, pairs)),
        ],
        compiler_params=pltpu.CompilerParams(
            collective_id=0, has_side_effects=True, vmem_limit_bytes=40 * 1024 * 1024
        ),
        name="render",
    )(density, palette, light_dir, slab_of)


def solution(mesh):
    in_specs = (P("depth", "tile", None), P(), P(), P())
    out_specs = P(None, None, "tile", "depth")
    body = functools.partial(on_device, mesh.shape["depth"], mesh.shape["tile"])
    return jax.shard_map(
        body, mesh=mesh, in_specs=in_specs, out_specs=out_specs, check_vma=False
    )
```

time: 163 us -> 30.6 us (0.19)
  other arithmetic: 80.9 us -> 0 us
  local copies, waits for them, and re-layouts: 54 us -> 6.19 us
  Pallas kernels: 0 us -> 24.2 us
  starting transfers between devices: 13.7 us -> 0 us
  waiting for transfers between devices: 9.26 us -> 0 us
  between operations: 4.11 us -> 0.01 us
    another operation x5 -> x0, other arithmetic: 32.7 us -> none  [the longest x1 30.6 us: march(): running = jnp.cumsum(optical, axis=0)]
    reduce_sum x2 -> x0, other arithmetic: 31.6 us -> none  [the longest x1 31.4 us: march(): plain = jnp.sum(weight, axis=0)]
    slice x7 -> x0, local copies, waits for them, and re-layouts: 25.6 us -> none  [the longest x2 19.4 us: centred(): lax.slice_in_dim(field, 1, size, axis=axis)]
    pallas_call x0 -> x1, Pallas kernels: none -> 24.2 us  [on_device(): pl.pallas_call(functools.partial(kernel, geom), out_shape=jax.ShapeDtypeS...]
    unnamed x2 -> x0, other arithmetic: 12.5 us -> none
    all_to_all x2 -> x0, starting transfers between devices: 9.36 us -> none  [the longest x1 5.16 us: on_device(): lax.all_to_all(slab_tau[None, None, None], 'depth', split_axis=4, concat_...]
    all_to_all x2 -> x0, waiting for transfers between devices: 9.25 us -> none  [the longest x1 9.25 us: on_device(): lax.all_to_all(slab_rgb[None], 'depth', split_axis=4, concat_axis=0, tile...]
    another operation x1 -> x0, local copies, waits for them, and re-layouts: 7.54 us -> none  [march(): jnp.stack(colours).astype(jnp.bfloat16)]
  transfers between devices with their start and end apart: 4 -> 0, of which waited for: 1 -> 0; matrix products, arithmetic and copies ran while one was open for 42% -> 0% of each run, Pallas kernels for 0% -> 0%
where the time goes in v1:
time: 30.6 us; the launch traced here: 30.4 us
  Pallas kernels  24.2 us (79%)
  local copies, waits for them, and re-layouts  6.19 us (20%)
    pallas_call x1, Pallas kernels, on_device(): pl.pallas_call(functools.partial(kernel, geom), out_shape=jax.ShapeDtypeS...  24.2 us
    unnamed x9, local copies, waits for them, and re-layouts  6.19 us

profile of v1, /device:TPU:0, one launch (start us, length us, event | category | flops | bytes accessed | tf_op | source)
XLA Modules:
  0.0 30.4 jit_solution(18382536360406885219)
XLA Ops:
  0.0 0.0 copy-start
  0.0 3.4 %copy-done = f32[32,32,2048]{2,1,0:T(8,128)S(1)} copy-done((f32[32,32,2048]{2,1,0:T(8,128)S(1)}, f32[32,32,2048]{2,1,0:T(8,128)}, u32[]{:S(2)}) %copy-start) | copy-done | bytes 8388632
  3.4 0.0 copy-start.1
  3.4 0.7 %copy-done.1 = f32[2,3]{1,0:T(2,128)S(1)} copy-done((f32[2,3]{1,0:T(2,128)S(1)}, f32[2,3]{1,0:T(2,128)}, u32[]{:S(2)}) %copy-start.1) | copy-done | bytes 48
  4.1 0.0 copy-start.2
  4.1 0.7 %copy-done.2 = f32[2,3]{1,0:T(2,128)S(1)} copy-done((f32[2,3]{1,0:T(2,128)S(1)}, f32[2,3]{1,0:T(2,128)}, u32[]{:S(2)}) %copy-start.2) | copy-done | bytes 48
  4.7 0.0 copy-start.3
  4.7 0.7 %copy-done.3 = s32[4]{0:T(128)S(1)} copy-done((s32[4]{0:T(128)S(1)}, s32[4]{0:T(128)}, u32[]{:S(2)}) %copy-start.3) | copy-done | bytes 40
  5.4 24.2 %render.1 = f32[2,4,32,512]{3,2,1,0:T(8,128)S(1)} custom-call(f32[32,32,2048]{2,1,0:T(8,128)S(1)} %copy-done, f32[2,3]{1,0:T(2,128)S(1)} %copy-done.1, f32[2,3]{1,0:T(2,128)S(1)} %copy-done.2, s32[4]{0:T(128)S(1)} %copy-done.3), custom_call_target="tpu_custom_call" | custom-call | tf_op jit(solution)/shard_map/render/pallas_call | solution.py:291
  29.6 0.8 %copy.6 = f32[2,4,32,512]{3,2,1,0:T(8,128)} copy(f32[2,4,32,512]{3,2,1,0:T(8,128)S(1)} %render.1) | data formatting | bytes 1048576
Async XLA Ops:
  0.0 3.4 %copy-start = (f32[32,32,2048]{2,1,0:T(8,128)S(1)}, f32[32,32,2048]{2,1,0:T(8,128)}, u32[]{:S(2)}) copy-start(f32[32,32,2048]{2,1,0:T(8,128)} %density.1) | copy-start | bytes 25165828
  3.4 0.7 %copy-start.1 = (f32[2,3]{1,0:T(2,128)S(1)}, f32[2,3]{1,0:T(2,128)}, u32[]{:S(2)}) copy-start(f32[2,3]{1,0:T(2,128)} %palette.1) | copy-start | bytes 76
  4.1 0.7 %copy-start.2 = (f32[2,3]{1,0:T(2,128)S(1)}, f32[2,3]{1,0:T(2,128)}, u32[]{:S(2)}) copy-start(f32[2,3]{1,0:T(2,128)} %light.1) | copy-start | bytes 76
  4.7 0.7 %copy-start.3 = (s32[4]{0:T(128)S(1)}, s32[4]{0:T(128)}, u32[]{:S(2)}) copy-start(s32[4]{0:T(128)} %slab_of.1) | copy-start | bytes 52

commit v2 on v1

--- a/solution.py
+++ b/solution.py
@@ -49,7 +49,7 @@
     def load(j):
         return pltpu.make_async_copy(
             density.at[:, :, pl.ds(j * LANES, LANES)],
-            buf.at[:, j, pl.ds(PAD, xs), :],
+            buf.at[:, j + 1, pl.ds(PAD, xs), :],
             load_sem.at[j],
         )
 
@@ -63,7 +63,7 @@
         source, row = ((xs - 1, low_row), (0, high_row))[side]
         return pltpu.make_async_remote_copy(
             src_ref=density.at[:, pl.ds(source, 1), pl.ds(j * LANES, LANES)],
-            dst_ref=buf.at[:, j, pl.ds(row, 1), :],
+            dst_ref=buf.at[:, j + 1, pl.ds(row, 1), :],
             send_sem=halo_send.at[side, j],
             recv_sem=halo_recv.at[side, j],
             device_id={"tile": target},
@@ -74,7 +74,7 @@
         source, row = ((0, low_row), (xs - 1, high_row))[side]
         return pltpu.make_async_copy(
             density.at[:, pl.ds(source, 1), pl.ds(j * LANES, LANES)],
-            buf.at[:, j, pl.ds(row, 1), :],
+            buf.at[:, j + 1, pl.ds(row, 1), :],
             halo_recv.at[side, j],
         )
 
@@ -100,44 +100,50 @@
 
     for j in range(tiles):
         load(j).wait()
+
+    def pad_columns(z, _):
+        for x0 in range(0, xs, SUB):
+            here = pl.ds(PAD + x0, SUB)
+            buf[z, 0, here, :] = pltpu.roll(buf[z, 1, here, :], LANES - 1, 1)
+            buf[z, tiles + 1, here, :] = pltpu.roll(buf[z, tiles, here, :], 1, 1)
+        return 0
+
+    lax.fori_loop(0, rows, pad_columns, 0, unroll=4)
 
     factor = 3.0 / (rows * depth_n)
     scale = factor * math.log2(math.e)
     lights = [[light[v, c] for c in range(3)] for v in range(2)]
     colours = [[palette[a, c] for c in range(3)] for a in range(2)]
     lane = lax.broadcasted_iota(jnp.int32, (group, SUB, LANES), 2)
-    place = lax.broadcasted_iota(jnp.int32, (group, SUB, LANES), 0)
     first, last = lane == 0, lane == LANES - 1
 
     def sweep(j0, x0, stag_j, stag_row):
-        end_low = first & (place == 0) & (j0 == 0)
-        end_high = last & (place == group - 1) & (j0 + group == tiles)
-        j_low = jnp.maximum(j0 - 1, 0)
-        j_high = jnp.minimum(j0 + group, tiles - 1)
         here = pl.ds(pl.multiple_of(x0 + PAD, SUB), SUB)
 
         def at(z, offset=0):
-            return buf[z, pl.ds(j0, group), pl.ds(x0 + PAD + offset, SUB), :]
+            where = pl.ds(x0 + PAD + offset, SUB) if offset else here
+            return buf[z, pl.ds(j0 + 1, group), where, :]
 
         def block(step, carry):
             run, seen, grown, p0, d0, p1, d1 = carry
             z0 = step * unroll
-            below = at(jnp.maximum(z0 - 1, 0))
+            below = at(max(z0 - 1, 0) if unroll == rows else jnp.maximum(z0 - 1, 0))
             mid = at(z0)
             for i in range(unroll):
                 z = z0 + i
-                above = at(jnp.minimum(z + 1, rows - 1) if i == unroll - 1 else z + 1)
+                if unroll == rows:
+                    above = at(min(z + 1, rows - 1))
+                else:
+                    above = at(jnp.minimum(z + 1, rows - 1) if i == unroll - 1 else z + 1)
                 gz = above - below
                 gx = at(z, 1) - at(z, -1)
-                edge_low = buf[z, pl.ds(j_low, 1), here, :]
-                edge_high = buf[z, pl.ds(j_high, 1), here, :]
+                edge_low = buf[z, pl.ds(j0, 1), here, :]
+                edge_high = buf[z, pl.ds(j0 + group + 1, 1), here, :]
                 if group > 1:
                     edge_low = jnp.concatenate([edge_low, mid[:-1]], 0)
                     edge_high = jnp.concatenate([mid[1:], edge_high], 0)
                 prior = pltpu.roll(jnp.where(last, edge_low, mid), 1, 2)
                 after = pltpu.roll(jnp.where(first, edge_high, mid), LANES - 1, 2)
-                prior = jnp.where(end_low, mid, prior)
-                after = jnp.where(end_high, mid, after)
                 gy = after - prior
                 inverse = lax.rsqrt(gx * gx + gy * gy + (gz * gz + 1.0))
                 shades = [
@@ -159,9 +165,12 @@
 
         zero = jnp.zeros((group, SUB, LANES), jnp.float32)
         one = jnp.ones((group, SUB, LANES), jnp.float32)
-        run, seen, _, p0, d0, p1, d1 = lax.fori_loop(
-            0, rows // unroll, block, (zero, one, one, zero, zero, zero, zero)
-        )
+        carry = (zero, one, one, zero, zero, zero, zero)
+        if unroll == rows:
+            carry = block(0, carry)
+        else:
+            carry = lax.fori_loop(0, rows // unroll, block, carry)
+        run, seen, _, p0, d0, p1, d1 = carry
         p1, d1 = p1 * seen, d1 * seen
         fields = [colours[0][c] * p0 + colours[1][c] * d0 for c in range(3)]
         fields += [colours[0][c] * p1 + colours[1][c] * d1 for c in range(3)]
@@ -205,6 +214,10 @@
         )
 
     pairs = xs // UNIT
+
+    def rows_of(u):
+        return (0, xs - SUB) if u == pairs - 1 else (SUB + u * UNIT, SUB)
+
     for u in range(pairs):
         if u == pairs - 1:
             for j in range(tiles):
@@ -218,23 +231,18 @@
                     def _(j=j, side=side):
                         halo_own(j, side).wait()
 
-        if u == pairs - 1:
-            x_first, x_step = 0, xs - SUB
-        else:
-            x_first, x_step = SUB + u * UNIT, SUB
         for step in range(depth_n - 1, 0, -1):
-            unit(partner(me, step, depth_n), x_first, x_step, send.at[step - 1, u])
+            unit(partner(me, step, depth_n), *rows_of(u), send.at[step - 1, u])
             outgoing(step, u).start()
-        unit(me, x_first, x_step, recv.at[me, u])
+
+    for u in range(pairs):
+        unit(me, *rows_of(u), recv.at[me, u])
 
     order = [slab_of[k] for k in range(depth_n)]
     for u in range(pairs):
         for step in range(1, depth_n):
             incoming(partner(me, step, depth_n), u).wait_recv()
-        if u == pairs - 1:
-            x_first, x_step = 0, xs - SUB
-        else:
-            x_first, x_step = SUB + u * UNIT, SUB
+        x_first, x_step = rows_of(u)
 
         def compose(j, _):
             cols = pl.ds(pl.multiple_of(j * LANES, LANES), LANES)
@@ -283,7 +291,7 @@
     tiles = ncols // LANES
     tiles_per = tiles // depth_n
     group = 2 if tiles_per % 2 == 0 else 1
-    unroll = 16
+    unroll = rows
     geom = (rows, xs, ncols, depth_n, tile_n, tiles_per, group, unroll)
     pairs = xs // UNIT
     cols = ncols // depth_n
@@ -294,7 +302,7 @@
         in_specs=[pl.BlockSpec(memory_space=pl.ANY), smem, smem, smem],
         out_specs=pl.BlockSpec(memory_space=pltpu.VMEM),
         scratch_shapes=[
-            pltpu.VMEM((rows, tiles, xs + 2 * PAD, LANES), jnp.float32),
+            pltpu.VMEM((rows, tiles + 2, xs + 2 * PAD, LANES), jnp.float32),
             pltpu.VMEM((7, tiles_per, UNIT, LANES), jnp.float32),
             pltpu.VMEM((depth_n - 1, pairs, 7, UNIT, cols), jnp.bfloat16),
             pltpu.VMEM((depth_n, pairs, 7, UNIT, cols), jnp.bfloat16),
@@ -305,7 +313,7 @@
             pltpu.SemaphoreType.DMA((depth_n, pairs)),
         ],
         compiler_params=pltpu.CompilerParams(
-            collective_id=0, has_side_effects=True, vmem_limit_bytes=40 * 1024 * 1024
+            collective_id=0, has_side_effects=True, vmem_limit_bytes=64 * 1024 * 1024
         ),
         name="render",
     )(density, palette, light_dir, slab_of)

time: 30.6 us -> 25.4 us (0.83)
  local copies, waits for them, and re-layouts: 6.19 us -> 1.87 us
  Pallas kernels: 24.2 us -> 23.4 us
    unnamed x9 -> x1, local copies, waits for them, and re-layouts: 6.19 us -> 1.87 us
    pallas_call x1, Pallas kernels: 24.2 us -> 23.4 us  [on_device(): pl.pallas_call(functools.partial(kernel, geom), out_shape=jax.ShapeDtypeS...]
where the time goes in v2:
time: 25.4 us; the launch traced here: 25.2 us
  Pallas kernels  23.4 us (92%)
  local copies, waits for them, and re-layouts  1.87 us (7%)
    pallas_call x1, Pallas kernels, on_device(): pl.pallas_call(functools.partial(kernel, geom), out_shape=jax.ShapeDtypeS...  23.4 us
    unnamed x1, local copies, waits for them, and re-layouts  1.87 us

profile of v2, /device:TPU:0, one launch (start us, length us, event | category | flops | bytes accessed | tf_op | source)
XLA Modules:
  0.0 25.2 jit_solution(14713492531507121328)
XLA Ops:
  0.0 23.4 %render.1 = f32[2,4,32,512]{3,2,1,0:T(8,128)} custom-call(f32[32,32,2048]{2,1,0:T(8,128)} %density.1, f32[2,3]{1,0:T(2,128)} %palette.1, f32[2,3]{1,0:T(2,128)} %light.1, s32[4]{0:T(128)} %slab_of.1), custom_call_target="tpu_custom_call" | custom-call | tf_op jit(solution)/shard_map/render/pallas_call | solution.py:299
  23.4 1.9 %copy.6 = f32[2,4,32,512]{3,2,1,0:T(8,128)} copy(f32[2,4,32,512]{3,2,1,0:T(8,128)} %render.1) | data formatting | bytes 1048576

commit v3 on v2

--- a/solution.py
+++ b/solution.py
@@ -26,7 +26,7 @@
 
 
 def kernel(
-    geom, density, palette, light, slab_of, out, buf, stag, send, recv,
+    geom, density, planes, palette, light, slab_of, out, buf, stag, send, recv,
     load_sem, halo_send, halo_recv, send_sem, recv_sem,
 ):
     rows, xs, ncols, depth_n, tile_n, tiles_per, group, unroll = geom
@@ -46,69 +46,88 @@
             barrier, inc=1, device_id={"tile": side}, device_id_type=pl.DeviceIdType.MESH
         )
 
-    def load(j):
+    def chunk_of(step):
+        return partner(me, step, depth_n) if step else me
+
+    steps = list(range(depth_n - 1, -1, -1))
+
+    def load(step, i):
+        chunk = chunk_of(step)
+        j = jnp.clip(chunk * tiles_per + i - 1, 0, tiles - 1)
         return pltpu.make_async_copy(
-            density.at[:, :, pl.ds(j * LANES, LANES)],
-            buf.at[:, j + 1, pl.ds(PAD, xs), :],
-            load_sem.at[j],
-        )
-
-    for j in range(tiles):
-        load(j).start()
+            density.at[:, :, pl.ds(pl.multiple_of(j * LANES, LANES), LANES)],
+            buf.at[:, chunk, i, pl.ds(PAD, xs), :],
+            load_sem.at[step, i],
+        )
+
+    def start_loads(step):
+        for i in range(tiles_per + 2):
+            load(step, i).start()
+
+    def finish_loads(step):
+        for i in range(tiles_per + 2):
+            load(step, i).wait()
+        chunk = chunk_of(step)
+
+        def pad_columns(z, own, pad, shift):
+            for x0 in range(0, xs, SUB):
+                here = pl.ds(PAD + x0, SUB)
+                buf[z, chunk, pad, here, :] = pltpu.roll(buf[z, chunk, own, here, :], shift, 1)
+
+        @pl.when(chunk == 0)
+        def _():
+            @pl.loop(0, rows, step=4)
+            def _(z):
+                for i in range(4):
+                    pad_columns(z + i, 1, 0, LANES - 1)
+
+        @pl.when(chunk == depth_n - 1)
+        def _():
+            @pl.loop(0, rows, step=4)
+            def _(z):
+                for i in range(4):
+                    pad_columns(z + i, tiles_per, tiles_per + 1, 1)
+
+    start_loads(steps[0])
     pl.semaphore_wait(barrier, depth_n + 1)
 
     low_row, high_row = PAD - 1, PAD + xs
 
-    def halo_to(j, side, target):
-        source, row = ((xs - 1, low_row), (0, high_row))[side]
+    def halo_part(source, row):
+        return (
+            planes.at[:, source // SUB, :, :, pl.ds(source % SUB, 1), :],
+            buf.at[:, :, pl.ds(1, tiles_per), pl.ds(row, 1), :],
+        )
+
+    def halo_to(side):
+        src, dst = halo_part(*((xs - 1, low_row), (0, high_row))[side])
         return pltpu.make_async_remote_copy(
-            src_ref=density.at[:, pl.ds(source, 1), pl.ds(j * LANES, LANES)],
-            dst_ref=buf.at[:, j + 1, pl.ds(row, 1), :],
-            send_sem=halo_send.at[side, j],
-            recv_sem=halo_recv.at[side, j],
-            device_id={"tile": target},
+            src_ref=src,
+            dst_ref=dst,
+            send_sem=halo_send.at[side],
+            recv_sem=halo_recv.at[side],
+            device_id={"tile": (right, left)[side]},
             device_id_type=pl.DeviceIdType.MESH,
         )
 
-    def halo_own(j, side):
-        source, row = ((0, low_row), (xs - 1, high_row))[side]
-        return pltpu.make_async_copy(
-            density.at[:, pl.ds(source, 1), pl.ds(j * LANES, LANES)],
-            buf.at[:, j + 1, pl.ds(row, 1), :],
-            halo_recv.at[side, j],
-        )
-
-    @pl.when(tile < tile_n - 1)
-    def _():
-        for j in range(tiles):
-            halo_to(j, 0, right).start()
-
-    @pl.when(tile > 0)
-    def _():
-        for j in range(tiles):
-            halo_to(j, 1, left).start()
-
-    @pl.when(tile == 0)
-    def _():
-        for j in range(tiles):
-            halo_own(j, 0).start()
-
-    @pl.when(tile == tile_n - 1)
-    def _():
-        for j in range(tiles):
-            halo_own(j, 1).start()
-
-    for j in range(tiles):
-        load(j).wait()
-
-    def pad_columns(z, _):
-        for x0 in range(0, xs, SUB):
-            here = pl.ds(PAD + x0, SUB)
-            buf[z, 0, here, :] = pltpu.roll(buf[z, 1, here, :], LANES - 1, 1)
-            buf[z, tiles + 1, here, :] = pltpu.roll(buf[z, tiles, here, :], 1, 1)
-        return 0
-
-    lax.fori_loop(0, rows, pad_columns, 0, unroll=4)
+    def halo_own(side):
+        src, dst = halo_part(*((0, low_row), (xs - 1, high_row))[side])
+        return pltpu.make_async_copy(src, dst, halo_recv.at[side])
+
+    for side, (sends, has) in enumerate(
+        ((tile < tile_n - 1, tile > 0), (tile > 0, tile < tile_n - 1))
+    ):
+
+        @pl.when(sends)
+        def _(side=side):
+            halo_to(side).start()
+
+        @pl.when(jnp.logical_not(has))
+        def _(side=side):
+            halo_own(side).start()
+
+    for step in steps[1:]:
+        start_loads(step)
 
     factor = 3.0 / (rows * depth_n)
     scale = factor * math.log2(math.e)
@@ -117,12 +136,12 @@
     lane = lax.broadcasted_iota(jnp.int32, (group, SUB, LANES), 2)
     first, last = lane == 0, lane == LANES - 1
 
-    def sweep(j0, x0, stag_j, stag_row):
+    def sweep(chunk, j0, x0, stag_j, stag_row):
         here = pl.ds(pl.multiple_of(x0 + PAD, SUB), SUB)
 
         def at(z, offset=0):
             where = pl.ds(x0 + PAD + offset, SUB) if offset else here
-            return buf[z, pl.ds(j0 + 1, group), where, :]
+            return buf[z, chunk, pl.ds(j0 + 1, group), where, :]
 
         def block(step, carry):
             run, seen, grown, p0, d0, p1, d1 = carry
@@ -137,8 +156,8 @@
                     above = at(jnp.minimum(z + 1, rows - 1) if i == unroll - 1 else z + 1)
                 gz = above - below
                 gx = at(z, 1) - at(z, -1)
-                edge_low = buf[z, pl.ds(j0, 1), here, :]
-                edge_high = buf[z, pl.ds(j0 + group + 1, 1), here, :]
+                edge_low = buf[z, chunk, pl.ds(j0, 1), here, :]
+                edge_high = buf[z, chunk, pl.ds(j0 + group + 1, 1), here, :]
                 if group > 1:
                     edge_low = jnp.concatenate([edge_low, mid[:-1]], 0)
                     edge_high = jnp.concatenate([mid[1:], edge_high], 0)
@@ -184,7 +203,7 @@
         def part(index, _):
             half, piece = index // groups, lax.rem(index, groups)
             sweep(
-                dest * tiles_per + piece * group, x_first + half * x_step, piece * group, half * SUB
+                dest, piece * group, x_first + half * x_step, piece * group, half * SUB
             )
             return 0
 
@@ -220,21 +239,23 @@
 
     for u in range(pairs):
         if u == pairs - 1:
-            for j in range(tiles):
-                for side, has in ((0, tile > 0), (1, tile < tile_n - 1)):
-
-                    @pl.when(has)
-                    def _(j=j, side=side):
-                        halo_to(j, side, (right, left)[side]).wait_recv()
-
-                    @pl.when(jnp.logical_not(has))
-                    def _(j=j, side=side):
-                        halo_own(j, side).wait()
-
-        for step in range(depth_n - 1, 0, -1):
+            for side, has in ((0, tile > 0), (1, tile < tile_n - 1)):
+
+                @pl.when(has)
+                def _(side=side):
+                    halo_to(side).wait_recv()
+
+                @pl.when(jnp.logical_not(has))
+                def _(side=side):
+                    halo_own(side).wait()
+
+        for step in steps[:-1]:
+            if u == 0:
+                finish_loads(step)
             unit(partner(me, step, depth_n), *rows_of(u), send.at[step - 1, u])
             outgoing(step, u).start()
 
+    finish_loads(0)
     for u in range(pairs):
         unit(me, *rows_of(u), recv.at[me, u])
 
@@ -275,15 +296,11 @@
     for u in range(pairs):
         for step in range(1, depth_n):
             outgoing(step, u).wait_send()
-    for j in range(tiles):
-
-        @pl.when(tile < tile_n - 1)
-        def _(j=j):
-            halo_to(j, 0, right).wait_send()
-
-        @pl.when(tile > 0)
-        def _(j=j):
-            halo_to(j, 1, left).wait_send()
+    for side, sends in enumerate((tile < tile_n - 1, tile > 0)):
+
+        @pl.when(sends)
+        def _(side=side):
+            halo_to(side).wait_send()
 
 
 def on_device(depth_n, tile_n, density, palette, light_dir, slab_of):
@@ -295,28 +312,30 @@
     geom = (rows, xs, ncols, depth_n, tile_n, tiles_per, group, unroll)
     pairs = xs // UNIT
     cols = ncols // depth_n
+    planes = density.reshape(rows, xs // SUB, SUB, depth_n, tiles_per, LANES)
+    planes = planes.transpose(0, 1, 3, 4, 2, 5)
     smem = pl.BlockSpec(memory_space=pltpu.SMEM)
     return pl.pallas_call(
         functools.partial(kernel, geom),
         out_shape=jax.ShapeDtypeStruct((2, 4, xs, cols), jnp.float32),
-        in_specs=[pl.BlockSpec(memory_space=pl.ANY), smem, smem, smem],
+        in_specs=[pl.BlockSpec(memory_space=pl.ANY)] * 2 + [smem, smem, smem],
         out_specs=pl.BlockSpec(memory_space=pltpu.VMEM),
         scratch_shapes=[
-            pltpu.VMEM((rows, tiles + 2, xs + 2 * PAD, LANES), jnp.float32),
+            pltpu.VMEM((rows, depth_n, tiles_per + 2, xs + 2 * PAD, LANES), jnp.float32),
             pltpu.VMEM((7, tiles_per, UNIT, LANES), jnp.float32),
             pltpu.VMEM((depth_n - 1, pairs, 7, UNIT, cols), jnp.bfloat16),
             pltpu.VMEM((depth_n, pairs, 7, UNIT, cols), jnp.bfloat16),
-            pltpu.SemaphoreType.DMA((tiles,)),
-            pltpu.SemaphoreType.DMA((2, tiles)),
-            pltpu.SemaphoreType.DMA((2, tiles)),
+            pltpu.SemaphoreType.DMA((depth_n, tiles_per + 2)),
+            pltpu.SemaphoreType.DMA((2,)),
+            pltpu.SemaphoreType.DMA((2,)),
             pltpu.SemaphoreType.DMA((depth_n - 1, pairs)),
             pltpu.SemaphoreType.DMA((depth_n, pairs)),
         ],
         compiler_params=pltpu.CompilerParams(
-            collective_id=0, has_side_effects=True, vmem_limit_bytes=64 * 1024 * 1024
+            collective_id=0, has_side_effects=True, vmem_limit_bytes=(64 * 1024 - 640) * 1024
         ),
         name="render",
-    )(density, palette, light_dir, slab_of)
+    )(density, planes, palette, light_dir, slab_of)
 
 
 def solution(mesh):

time: 25.4 us -> 24.4 us (0.961)
  Pallas kernels: 23.4 us -> 22.3 us
    pallas_call x1, Pallas kernels: 23.4 us -> 22.3 us  [on_device(): pl.pallas_call(functools.partial(kernel, geom), out_shape=jax.ShapeDtypeS...]
where the time goes in v3:
time: 24.4 us; the launch traced here: 24.2 us
  Pallas kernels  22.3 us (91%)
  local copies, waits for them, and re-layouts  1.87 us (8%)
    pallas_call x1, Pallas kernels, on_device(): pl.pallas_call(functools.partial(kernel, geom), out_shape=jax.ShapeDtypeS...  22.3 us
    unnamed x1, local copies, waits for them, and re-layouts  1.87 us

profile of v3, /device:TPU:0, one launch (start us, length us, event | category | flops | bytes accessed | tf_op | source)
XLA Modules:
  0.0 24.2 jit_solution(17103837546044338394)
XLA Ops:
  0.0 22.3 %render.1 = f32[2,4,32,512]{3,2,1,0:T(8,128)} custom-call(f32[32,32,2048]{2,1,0:T(8,128)} %density.1, f32[32,4,4,4,8,128]{5,4,3,2,1,0:T(8,128)} %bitcast.3, f32[2,3]{1,0:T(2,128)} %palette.1, f32[2,3]{1,0:T(2,128)} %light.1, s32[4]{0:T(128)} %slab_of.1), custom_call_target="tpu_custom_call" | custom-call | tf_op jit(solution)/shard_map/render/pallas_call | solution.py:318
  22.4 1.9 %copy.6 = f32[2,4,32,512]{3,2,1,0:T(8,128)} copy(f32[2,4,32,512]{3,2,1,0:T(8,128)} %render.1) | data formatting | bytes 1048576

commit v4 on v3

--- a/solution.py
+++ b/solution.py
@@ -20,7 +20,8 @@
     out, bit = 0, 1
     while bit < count:
         mine = lax.rem(me // bit, 2)
-        out = out + bit * (1 - mine if step & bit else mine)
+        flip = lax.rem(step // bit, 2)
+        out = out + bit * (mine + flip - 2 * mine * flip)
         bit *= 2
     return out
 
@@ -47,7 +48,7 @@
         )
 
     def chunk_of(step):
-        return partner(me, step, depth_n) if step else me
+        return partner(me, step, depth_n)
 
     steps = list(range(depth_n - 1, -1, -1))
 
@@ -195,19 +196,11 @@
         fields += [colours[0][c] * p1 + colours[1][c] * d1 for c in range(3)]
         fields.append(run * factor)
         for f, value in enumerate(fields):
-            stag[f, pl.ds(stag_j, group), pl.ds(pl.multiple_of(stag_row, SUB), SUB), :] = value
+            stag[f, pl.ds(stag_j, group), pl.ds(stag_row, SUB), :] = value
 
     groups = tiles_per // group
 
-    def unit(dest, x_first, x_step, target):
-        def part(index, _):
-            half, piece = index // groups, lax.rem(index, groups)
-            sweep(
-                dest, piece * group, x_first + half * x_step, piece * group, half * SUB
-            )
-            return 0
-
-        lax.fori_loop(0, 2 * groups, part, 0)
+    def store(target):
         for f in range(7):
             for j in range(tiles_per):
                 target[f, :, pl.ds(j * LANES, LANES)] = stag[f, j].astype(jnp.bfloat16)
@@ -237,27 +230,49 @@
     def rows_of(u):
         return (0, xs - SUB) if u == pairs - 1 else (SUB + u * UNIT, SUB)
 
-    for u in range(pairs):
-        if u == pairs - 1:
-            for side, has in ((0, tile > 0), (1, tile < tile_n - 1)):
-
-                @pl.when(has)
-                def _(side=side):
-                    halo_to(side).wait_recv()
-
-                @pl.when(jnp.logical_not(has))
-                def _(side=side):
-                    halo_own(side).wait()
-
-        for step in steps[:-1]:
-            if u == 0:
-                finish_loads(step)
-            unit(partner(me, step, depth_n), *rows_of(u), send.at[step - 1, u])
+    remote = pairs * (depth_n - 1)
+
+    def unit(t, _):
+        own = t >= remote
+        u = jnp.where(own, t - remote, t // (depth_n - 1))
+        step = jnp.where(own, 0, depth_n - 1 - lax.rem(t, depth_n - 1))
+
+        @pl.when((t < depth_n - 1) | (t == remote))
+        def _():
+            finish_loads(step)
+
+        for side, has in ((0, tile > 0), (1, tile < tile_n - 1)):
+
+            @pl.when((t == (pairs - 1) * (depth_n - 1)) & has)
+            def _(side=side):
+                halo_to(side).wait_recv()
+
+            @pl.when((t == (pairs - 1) * (depth_n - 1)) & jnp.logical_not(has))
+            def _(side=side):
+                halo_own(side).wait()
+
+        outer = u == pairs - 1
+        x_first = jnp.where(outer, 0, SUB + u * UNIT)
+        x_step = jnp.where(outer, xs - SUB, SUB)
+        dest = chunk_of(step)
+        for half in range(2):
+            for piece in range(groups):
+                sweep(
+                    dest, piece * group, x_first + half * x_step, piece * group, half * SUB
+                )
+
+        @pl.when(own)
+        def _():
+            store(recv.at[me, u])
+
+        @pl.when(jnp.logical_not(own))
+        def _():
+            store(send.at[step - 1, u])
             outgoing(step, u).start()
 
-    finish_loads(0)
-    for u in range(pairs):
-        unit(me, *rows_of(u), recv.at[me, u])
+        return 0
+
+    lax.fori_loop(0, remote + pairs, unit, 0)
 
     order = [slab_of[k] for k in range(depth_n)]
     for u in range(pairs):

time: 24.4 us -> 23.9 us (0.980)
  Pallas kernels: 22.3 us -> 21.9 us
    pallas_call x1, Pallas kernels: 22.3 us -> 21.9 us  [on_device(): pl.pallas_call(functools.partial(kernel, geom), out_shape=jax.ShapeDtypeS...]
where the time goes in v4:
time: 23.9 us; the launch traced here: 23.8 us
  Pallas kernels  21.9 us (92%)
  local copies, waits for them, and re-layouts  1.87 us (8%)
    pallas_call x1, Pallas kernels, on_device(): pl.pallas_call(functools.partial(kernel, geom), out_shape=jax.ShapeDtypeS...  21.9 us
    unnamed x1, local copies, waits for them, and re-layouts  1.87 us

profile of v4, /device:TPU:0, one launch (start us, length us, event | category | flops | bytes accessed | tf_op | source)
XLA Modules:
  0.0 23.8 jit_solution(3289722822268346900)
XLA Ops:
  0.0 21.9 %render.1 = f32[2,4,32,512]{3,2,1,0:T(8,128)} custom-call(f32[32,32,2048]{2,1,0:T(8,128)} %density.1, f32[32,4,4,4,8,128]{5,4,3,2,1,0:T(8,128)} %bitcast.3, f32[2,3]{1,0:T(2,128)} %palette.1, f32[2,3]{1,0:T(2,128)} %light.1, s32[4]{0:T(128)} %slab_of.1), custom_call_target="tpu_custom_call" | custom-call | tf_op jit(solution)/shard_map/render/pallas_call | solution.py:333
  21.9 1.9 %copy.6 = f32[2,4,32,512]{3,2,1,0:T(8,128)} copy(f32[2,4,32,512]{3,2,1,0:T(8,128)} %render.1) | data formatting | bytes 1048576

commit v5 on v4

--- a/solution.py
+++ b/solution.py
@@ -89,8 +89,8 @@
                 for i in range(4):
                     pad_columns(z + i, tiles_per, tiles_per + 1, 1)
 
-    start_loads(steps[0])
-    pl.semaphore_wait(barrier, depth_n + 1)
+    for step in steps:
+        start_loads(step)
 
     low_row, high_row = PAD - 1, PAD + xs
 
@@ -115,20 +115,18 @@
         src, dst = halo_part(*((0, low_row), (xs - 1, high_row))[side])
         return pltpu.make_async_copy(src, dst, halo_recv.at[side])
 
-    for side, (sends, has) in enumerate(
-        ((tile < tile_n - 1, tile > 0), (tile > 0, tile < tile_n - 1))
-    ):
-
-        @pl.when(sends)
-        def _(side=side):
-            halo_to(side).start()
-
-        @pl.when(jnp.logical_not(has))
-        def _(side=side):
-            halo_own(side).start()
-
-    for step in steps[1:]:
-        start_loads(step)
+    def start_halo():
+        for side, (sends, has) in enumerate(
+            ((tile < tile_n - 1, tile > 0), (tile > 0, tile < tile_n - 1))
+        ):
+
+            @pl.when(sends)
+            def _(side=side):
+                halo_to(side).start()
+
+            @pl.when(jnp.logical_not(has))
+            def _(side=side):
+                halo_own(side).start()
 
     factor = 3.0 / (rows * depth_n)
     scale = factor * math.log2(math.e)
@@ -232,6 +230,13 @@
 
     remote = pairs * (depth_n - 1)
 
+    def meet():
+        pl.semaphore_wait(barrier, depth_n + 1)
+        start_halo()
+
+    if pairs == 1:
+        meet()
+
     def unit(t, _):
         own = t >= remote
         u = jnp.where(own, t - remote, t // (depth_n - 1))
@@ -260,6 +265,9 @@
                 sweep(
                     dest, piece * group, x_first + half * x_step, piece * group, half * SUB
                 )
+
+        if pairs > 1:
+            pl.when(t == 0)(meet)
 
         @pl.when(own)
         def _():

time: 23.9 us -> 24.1 us (level)
  the two profiles are of different devices: /device:TPU:0 before, /device:TPU:1 now
where the time goes in v5:
time: 24.1 us; the launch traced here: 24 us
  Pallas kernels  22.1 us (92%)
  local copies, waits for them, and re-layouts  1.87 us (8%)
    pallas_call x1, Pallas kernels, on_device(): pl.pallas_call(functools.partial(kernel, geom), out_shape=jax.ShapeDtypeS...  22.1 us
    unnamed x1, local copies, waits for them, and re-layouts  1.87 us

profile of v5, /device:TPU:1, one launch (start us, length us, event | category | flops | bytes accessed | tf_op | source)
XLA Modules:
  0.0 24.0 jit_solution(9515077638765348386)
XLA Ops:
  0.0 22.1 %render.1 = f32[2,4,32,512]{3,2,1,0:T(8,128)} custom-call(f32[32,32,2048]{2,1,0:T(8,128)} %density.1, f32[32,4,4,4,8,128]{5,4,3,2,1,0:T(8,128)} %bitcast.3, f32[2,3]{1,0:T(2,128)} %palette.1, f32[2,3]{1,0:T(2,128)} %light.1, s32[4]{0:T(128)} %slab_of.1), custom_call_target="tpu_custom_call" | custom-call | tf_op jit(solution)/shard_map/render/pallas_call | solution.py:341
  22.1 1.9 %copy.6 = f32[2,4,32,512]{3,2,1,0:T(8,128)} copy(f32[2,4,32,512]{3,2,1,0:T(8,128)} %render.1) | data formatting | bytes 1048576

commit v6 on v5

--- a/solution.py
+++ b/solution.py
@@ -143,7 +143,7 @@
             return buf[z, chunk, pl.ds(j0 + 1, group), where, :]
 
         def block(step, carry):
-            run, seen, grown, p0, d0, p1, d1 = carry
+            run, seen, p0, d0, p1, d1 = carry
             z0 = step * unroll
             below = at(max(z0 - 1, 0) if unroll == rows else jnp.maximum(z0 - 1, 0))
             mid = at(z0)
@@ -168,28 +168,27 @@
                     jnp.abs(gx * l[0] + gy * l[1] + gz * l[2]) * inverse + 0.3 for l in lights
                 ]
                 run = run + mid
-                power = run * scale
-                seen_next = jnp.exp2(-power)
-                grown_next = jnp.exp2(power)
-                c0 = (seen - seen_next) * shades[0]
-                c1 = (grown_next - grown) * shades[1]
+                passed = jnp.exp2(mid * -scale)
+                opacity = 1.0 - passed
+                taken = seen * opacity
+                seen = seen - taken
+                c0 = taken * shades[0]
+                c1 = opacity * shades[1]
                 p0 = p0 + c0
                 d0 = d0 + mid * c0
-                p1 = p1 + c1
-                d1 = d1 + mid * c1
-                seen, grown = seen_next, grown_next
+                p1 = p1 * passed + c1
+                d1 = d1 * passed + mid * c1
                 below, mid = mid, above
-            return run, seen, grown, p0, d0, p1, d1
+            return run, seen, p0, d0, p1, d1
 
         zero = jnp.zeros((group, SUB, LANES), jnp.float32)
         one = jnp.ones((group, SUB, LANES), jnp.float32)
-        carry = (zero, one, one, zero, zero, zero, zero)
+        carry = (zero, one, zero, zero, zero, zero)
         if unroll == rows:
             carry = block(0, carry)
         else:
             carry = lax.fori_loop(0, rows // unroll, block, carry)
-        run, seen, _, p0, d0, p1, d1 = carry
-        p1, d1 = p1 * seen, d1 * seen
+        run, seen, p0, d0, p1, d1 = carry
         fields = [colours[0][c] * p0 + colours[1][c] * d0 for c in range(3)]
         fields += [colours[0][c] * p1 + colours[1][c] * d1 for c in range(3)]
         fields.append(run * factor)

time: 24.1 us -> 24.3 us (level)
  no operation moved by 1% of the time
where the time goes in v6:
time: 24.3 us; the launch traced here: 24.2 us
  Pallas kernels  22.3 us (92%)
  local copies, waits for them, and re-layouts  1.87 us (8%)
    pallas_call x1, Pallas kernels, on_device(): pl.pallas_call(functools.partial(kernel, geom), out_shape=jax.ShapeDtypeS...  22.3 us
    unnamed x1, local copies, waits for them, and re-layouts  1.87 us

profile of v6, /device:TPU:1, one launch (start us, length us, event | category | flops | bytes accessed | tf_op | source)
XLA Modules:
  0.0 24.2 jit_solution(16164548442216454171)
XLA Ops:
  0.0 22.3 %render.1 = f32[2,4,32,512]{3,2,1,0:T(8,128)} custom-call(f32[32,32,2048]{2,1,0:T(8,128)} %density.1, f32[32,4,4,4,8,128]{5,4,3,2,1,0:T(8,128)} %bitcast.3, f32[2,3]{1,0:T(2,128)} %palette.1, f32[2,3]{1,0:T(2,128)} %light.1, s32[4]{0:T(128)} %slab_of.1), custom_call_target="tpu_custom_call" | custom-call | tf_op jit(solution)/shard_map/render/pallas_call | solution.py:340
  22.3 1.9 %copy.6 = f32[2,4,32,512]{3,2,1,0:T(8,128)} copy(f32[2,4,32,512]{3,2,1,0:T(8,128)} %render.1) | data formatting | bytes 1048576

commit v7 on v5

--- a/solution.py
+++ b/solution.py
@@ -89,8 +89,7 @@
                 for i in range(4):
                     pad_columns(z + i, tiles_per, tiles_per + 1, 1)
 
-    for step in steps:
-        start_loads(step)
+    start_loads(steps[0])
 
     low_row, high_row = PAD - 1, PAD + xs
 
@@ -246,6 +245,11 @@
         def _():
             finish_loads(step)
 
+        @pl.when(t == 0)
+        def _():
+            for later in steps[1:]:
+                start_loads(later)
+
         for side, has in ((0, tile > 0), (1, tile < tile_n - 1)):
 
             @pl.when((t == (pairs - 1) * (depth_n - 1)) & has)

time: 24.1 us -> 24.2 us (level)
  no operation moved by 1% of the time
where the time goes in v7:
time: 24.2 us; the launch traced here: 24.1 us
  Pallas kernels  22.2 us (92%)
  local copies, waits for them, and re-layouts  1.87 us (8%)
    pallas_call x1, Pallas kernels, on_device(): pl.pallas_call(functools.partial(kernel, geom), out_shape=jax.ShapeDtypeS...  22.2 us
    unnamed x1, local copies, waits for them, and re-layouts  1.87 us

profile of v7, /device:TPU:1, one launch (start us, length us, event | category | flops | bytes accessed | tf_op | source)
XLA Modules:
  0.0 24.1 jit_solution(2936704788313955155)
XLA Ops:
  0.0 22.2 %render.1 = f32[2,4,32,512]{3,2,1,0:T(8,128)} custom-call(f32[32,32,2048]{2,1,0:T(8,128)} %density.1, f32[32,4,4,4,8,128]{5,4,3,2,1,0:T(8,128)} %bitcast.3, f32[2,3]{1,0:T(2,128)} %palette.1, f32[2,3]{1,0:T(2,128)} %light.1, s32[4]{0:T(128)} %slab_of.1), custom_call_target="tpu_custom_call" | custom-call | tf_op jit(solution)/shard_map/render/pallas_call | solution.py:345
  22.2 1.9 %copy.6 = f32[2,4,32,512]{3,2,1,0:T(8,128)} copy(f32[2,4,32,512]{3,2,1,0:T(8,128)} %render.1) | data formatting | bytes 1048576
